TPU v7x, 512 devices: a whole 4x4x16 slice. The times are simulated.
512 devices in a mesh: gx: 32 (over z, core), gy: 16 (over y, x).
Axes of the slice: x: 4, y: 4, z: 16, core: 2. Of those that a mesh axis runs over, the one named last changes fastest.
Arguments:
- charge_densities: float32 [2, 128, 512, 256], P(None, 'gx', 'gy'), may hold values from 0.2 to 5
- upwind_linkage: float32 [2, 2, 128, 512, 256], P(None, None, 'gx', 'gy'), may hold values from 0.1 to 1, as said below
- decay_duration: float32 [128, 512, 256], P('gx', 'gy'), may hold values from 0.3 to 3
- deposited_packets: float32 [32, 16, 32, 8, 128], P('gx', 'gy'), may hold values from 0.25 to 4
- active_packet_tally: int32 [32, 16, 32], P('gx', 'gy'), may hold values from 0 to 8, as said below
- receiving_packet_position: int32 [32, 16, 32, 8], P('gx', 'gy'), may hold values from 0 to 255
Outputs:
- updated: float32 [2, 128, 512, 256], P(None, 'gx', 'gy')
Inputs may be any that keep to these rules, and one draw needn't show every extreme that they name: `upwind_linkage`: its values lie strictly between 0 and 1. active_packet_tally[s, r, d] counts the live slots, the first ones, of the blocks from tile s to tile d in row r; it is at most 8 and reaches 8 in every draw.
All inputs are finite; a program needn't handle non-finite values.
Results may differ from a plain program's by a relative error of at most 0.000071.
Values sent between devices are 32-bit elements; how exact they have to be, the bound alone decides.
A program may use at most 64 MiB of HBM per device.

v0:
```python
import jax
import jax.numpy as jnp
from jax import lax
from jax.sharding import PartitionSpec as P

interval_duration = 0.5
intrinsic_sq = 0.01
trap_level = 0.1


def carried_in(part, axis, combine, identity, reverse):
    count = lax.axis_size(axis)
    place = lax.axis_index(axis)
    ahead = count - 1 - place if reverse else place
    gathered = jax.tree.map(lambda a: lax.all_gather(a, axis), part)
    state = jax.tree.map(lambda a, e: jnp.zeros_like(a) + jnp.asarray(e, a.dtype), part, identity)

    def one(lap, state):
        source = count - 1 - lap if reverse else lap
        return combine(
            state, jax.tree.map(lambda a: lax.dynamic_index_in_dim(a, source, 0, False), gathered)
        )

    return lax.fori_loop(0, ahead, one, state)


def compose(earlier, later):
    return (earlier[0] * later[0], later[0] * earlier[1] + later[1])


def prefix_region_sweep(values, coupling, dim):
    return lax.associative_scan(compose, (coupling, (1.0 - coupling) * values), axis=dim)


def backward_local(values, coupling, dim):
    return lax.associative_scan(
        compose, (coupling, (1.0 - coupling) * values), reverse=True, axis=dim
    )


def deposit(arrived, cell_shape):
    block_rows, sites_in, counts_in = arrived
    block_len = block_rows.shape[-1]
    capacity = block_rows.shape[1]
    site_total = cell_shape[0] * cell_shape[1] * (cell_shape[2] // block_len)
    live = (
        (jnp.arange(capacity, dtype=jnp.int32)[None, :] < counts_in[:, None])
        .astype(jnp.float32)
        .reshape(-1)
    )
    onehot = (
        sites_in.reshape(-1)[:, None] == jnp.arange(site_total, dtype=jnp.int32)[None, :]
    ).astype(jnp.float32)
    onehot = onehot * live[:, None]
    summed = lax.dot_general(
        onehot,
        block_rows.reshape(-1, block_len),
        (((0,), (0,)), ((), ())),
        precision=lax.Precision.HIGHEST,
        preferred_element_type=jnp.float32,
    )
    return summed.reshape(cell_shape)


def on_device(
    charge_densities,
    upwind_linkage,
    decay_duration,
    deposited_packets,
    active_packet_tally,
    receiving_packet_position,
):
    arrived = (
        lax.all_to_all(deposited_packets[0, 0], "gx", split_axis=0, concat_axis=0, tiled=True),
        lax.all_to_all(
            receiving_packet_position[0, 0], "gx", split_axis=0, concat_axis=0, tiled=True
        ),
        lax.all_to_all(active_packet_tally[0, 0], "gx", split_axis=0, concat_axis=0, tiled=True),
    )
    horizontal_direction_flag = upwind_linkage[0]
    along_y = upwind_linkage[1]
    prefix_multiplier, running_prefix = prefix_region_sweep(
        charge_densities, horizontal_direction_flag, 1
    )
    entering = carried_in(
        (prefix_multiplier[:, -1], running_prefix[:, -1]),
        "gx",
        compose,
        (jnp.ones_like(prefix_multiplier[:, -1]), jnp.zeros_like(running_prefix[:, -1])),
        False,
    )
    swept = running_prefix + prefix_multiplier * entering[1][:, None]
    prod_back, part_back = backward_local(swept, horizontal_direction_flag, 1)
    entering = carried_in(
        (prod_back[:, 0], part_back[:, 0]),
        "gx",
        compose,
        (jnp.ones_like(prod_back[:, 0]), jnp.zeros_like(part_back[:, 0])),
        True,
    )
    swept = part_back + prod_back * entering[1][:, None]
    prefix_multiplier, running_prefix = prefix_region_sweep(swept, along_y, 2)
    entering = carried_in(
        (prefix_multiplier[:, :, -1], running_prefix[:, :, -1]),
        "gy",
        compose,
        (jnp.ones_like(prefix_multiplier[:, :, -1]), jnp.zeros_like(running_prefix[:, :, -1])),
        False,
    )
    swept = running_prefix + prefix_multiplier * entering[1][:, :, None]
    prod_back, part_back = backward_local(swept, along_y, 2)
    entering = carried_in(
        (prod_back[:, :, 0], part_back[:, :, 0]),
        "gy",
        compose,
        (jnp.ones_like(prod_back[:, :, 0]), jnp.zeros_like(part_back[:, :, 0])),
        True,
    )
    swept = part_back + prod_back * entering[1][:, :, None]
    creation_source = deposit(arrived, decay_duration.shape)
    negative_population = swept[0]
    positive_population = swept[1]
    spread_coefficient = (negative_population * positive_population - intrinsic_sq) / (
        decay_duration
        * (3.0 * (negative_population + trap_level) + (positive_population + trap_level))
    )
    return swept + interval_duration * (creation_source - spread_coefficient)[None]


def solution(mesh):
    in_specs = (
        P(None, "gx", "gy", None),
        P(None, None, "gx", "gy", None),
        P("gx", "gy", None),
        P("gx", "gy", None, None, None),
        P("gx", "gy", None),
        P("gx", "gy", None, None),
    )
    out_specs = P(None, "gx", "gy", None)
    return jax.shard_map(
        on_device, mesh=mesh, in_specs=in_specs, out_specs=out_specs, check_vma=False
    )
```

profile of v0, /device:TPU:2, one launch (start us, length us, event | category | flops | bytes accessed | tf_op | source)
XLA Modules:
  0.0 460.2 jit_solution(983130188485720610)
XLA Ops:
  6.5 1.1 slice_bitcast_fusion
  7.6 1.1 subtract_multiply_fusion
  9.0 0.6 slice_add_fusion.4
  9.8 0.6 slice_add_fusion.5
  10.5 75.5 %all-gather.15.cloned.1.call-done = f32[64,1,32,256]{3,2,1,0:T(8,128)} async-done(((f32[2,1,32,256]{3,2,1,0:T(8,128)}), f32[64,1,32,256]{3,2,1,0:T(8,128)}) %all-gather.15.cloned.1.call-update) | async-done | bytes 2097168 | tf_op jit(solution)/shard_map/all_gather | solution.py:15
  86.0 70.8 %all-gather.13.cloned.1.call-done = f32[64,1,32,256]{3,2,1,0:T(8,128)} async-done(((f32[2,1,32,256]{3,2,1,0:T(8,128)}), f32[64,1,32,256]{3,2,1,0:T(8,128)}) %all-gather.13.cloned.1.call-update) | async-done | bytes 2097168 | tf_op jit(solution)/shard_map/all_gather | solution.py:15
  157.3 0.6 slice_add_fusion.1
  158.2 0.6 slice_add_fusion.2
  158.9 0.7 copy.19
  159.6 33.0 %all-to-all-start.1 = ((s32[32,1,1]{2,1,0:T(1,128)}), s32[32,1,1]{2,1,0:T(1,128)S(1)}, u32[]{:S(2)}, u32[]{:S(2)}) async-start(s32[32,1,1]{2,1,0:T(1,128)} %copy.19), calls=%async_computation.1 | async-start | bytes 32768 | tf_op jit(solution)/shard_map/all_to_all | solution.py:78
  192.7 12.3 %all-to-all-done.1 = s32[32,1,1]{2,1,0:T(1,128)S(1)} async-done(((s32[32,1,1]{2,1,0:T(1,128)}), s32[32,1,1]{2,1,0:T(1,128)S(1)}, u32[]{:S(2)}, u32[]{:S(2)}) %all-to-all-start.1) | async-done | bytes 160 | tf_op jit(solution)/shard_map/all_to_all | solution.py:78
  205.0 15.4 %all_to_all.23 = s32[32,1,8]{2,1,0:T(1,128)S(1)} all-to-all(s32[32,1,8]{2,1,0:T(1,128)S(1)} %bitcast.124), channel_id=1, replica_groups=mesh['gx'=32,'gy'=16] {'gx'}, dimensions={0} | all-to-all | bytes 2048 | tf_op jit(solution)/shard_map/all_to_all | solution.py:75
  220.5 3.9 all-to-all-start.2
  224.6 0.1 slice.485
  225.1 0.7 reduce.1
  226.0 0.6 broadcast.169
  226.5 0.7 reduce.4
  227.3 15.5 %all-to-all-done.2 = f32[32,8,128]{2,1,0:T(8,128)S(1)} async-done(((f32[32,8,128]{2,1,0:T(8,128)}), f32[32,8,128]{2,1,0:T(8,128)S(1)}, u32[]{:S(2)}, u32[]{:S(2)}) %all-to-all-start.2) | async-done | bytes 131104 | tf_op jit(solution)/shard_map/all_to_all | solution.py:74
  242.8 0.7 fusion
  243.6 10.2 %all-gather.19.cloned.1.call-done = f32[64,1,32,256]{3,2,1,0:T(8,128)} async-done(((f32[2,1,32,256]{3,2,1,0:T(8,128)}), f32[64,1,32,256]{3,2,1,0:T(8,128)}) %all-gather.19.cloned.1.call-update) | async-done | bytes 2097168 | tf_op jit(solution)/shard_map/all_gather | solution.py:15
  253.8 69.8 %all-gather.17.cloned.1.call-done = f32[64,1,32,256]{3,2,1,0:T(8,128)} async-done(((f32[2,1,32,256]{3,2,1,0:T(8,128)}), f32[64,1,32,256]{3,2,1,0:T(8,128)}) %all-gather.17.cloned.1.call-update) | async-done | bytes 2097168 | tf_op jit(solution)/shard_map/all_gather | solution.py:15
  323.6 28.8 %while.53 = (s32[]{:T(128)}, f32[2,32,256]{2,1,0:T(8,128)S(1)}, s32[]{:T(128)}, f32[32,2,32,256]{3,2,1,0:T(8,128)}, f32[32,2,32,256]{3,2,1,0:T(8,128)}, /*index=5*/s32[]{:T(128)}, s32[]{:T(128)}, s32[]{:T(128)}, s32[]{:T(128)}) while((s32[]{:T(128)}, f32[2,32,256]{2,1,0:T(8,128)S(1)}, s32[]{:T(128)}, f32[32,2,32,256]{3,2,1,0:T(8,128)}, ...), condition=%wide.region_3.4_spmd, body=%wide.region_2.3_spmd.sunk | while | flops 32774 | bytes 262287 | solution.py:24
  323.6 0.9 bitcast_add_fusion.9
  324.5 0.9 bitcast_add_fusion.9
  325.5 0.9 bitcast_add_fusion.9
  326.4 0.9 bitcast_add_fusion.9
  327.3 0.9 bitcast_add_fusion.9
  328.2 0.9 bitcast_add_fusion.9
  329.2 0.9 bitcast_add_fusion.9
  330.1 0.9 bitcast_add_fusion.9
  331.0 0.9 bitcast_add_fusion.9
  332.0 0.9 bitcast_add_fusion.9
  332.9 0.9 bitcast_add_fusion.9
  333.8 0.9 bitcast_add_fusion.9
  334.8 0.9 bitcast_add_fusion.9
  335.7 0.9 bitcast_add_fusion.9
  336.6 0.9 bitcast_add_fusion.9
  337.6 0.9 bitcast_add_fusion.9
  338.5 0.9 bitcast_add_fusion.9
  339.4 0.9 bitcast_add_fusion.9
  340.3 0.9 bitcast_add_fusion.9
  341.3 0.9 bitcast_add_fusion.9
  342.2 0.9 bitcast_add_fusion.9
  343.1 0.9 bitcast_add_fusion.9
  344.1 0.9 bitcast_add_fusion.9
  345.0 0.9 bitcast_add_fusion.9
  345.9 0.9 bitcast_add_fusion.9
  346.9 0.9 bitcast_add_fusion.9
  347.8 0.9 bitcast_add_fusion.9
  348.7 0.9 bitcast_add_fusion.9
  349.7 0.9 bitcast_add_fusion.9
  350.6 0.9 bitcast_add_fusion.9
  351.5 0.9 bitcast_add_fusion.9
  354.6 0.1 slice.518
  354.8 0.1 pad.204
  355.0 0.1 pad.194
  356.5 23.3 %all-gather.5 = f32[32,4,1,256]{3,1,2,0:T(4,128)S(1)} all-gather(f32[2,4,1,256]{3,1,2,0:T(4,128)S(1)} %copy.15), channel_id=7, replica_groups=mesh['gx'=32,'gy'=16] {'gy'}, dimensions={0}, use_global_device_ids=true | all-gather | bytes 139264 | tf_op jit(solution)/shard_map/all_gather | solution.py:15
  380.1 22.1 %all-gather.4 = f32[32,4,1,256]{3,1,2,0:T(4,128)S(1)} all-gather(f32[2,4,1,256]{3,1,2,0:T(4,128)S(1)} %copy.14), channel_id=6, replica_groups=mesh['gx'=32,'gy'=16] {'gy'}, dimensions={0}, use_global_device_ids=true | all-gather | bytes 139264 | tf_op jit(solution)/shard_map/all_gather | solution.py:15
  404.9 0.1 pad.214
  405.1 0.1 pad.224
  407.0 23.0 %all-gather.7 = f32[32,4,1,256]{3,1,2,0:T(4,128)S(1)} all-gather(f32[2,4,1,256]{3,1,2,0:T(4,128)S(1)} %copy.17), channel_id=9, replica_groups=mesh['gx'=32,'gy'=16] {'gy'}, dimensions={0}, use_global_device_ids=true | all-gather | bytes 139264 | tf_op jit(solution)/shard_map/all_gather | solution.py:15
  429.9 22.0 %all-gather.6 = f32[32,4,1,256]{3,1,2,0:T(4,128)S(1)} all-gather(f32[2,4,1,256]{3,1,2,0:T(4,128)S(1)} %copy.16), channel_id=8, replica_groups=mesh['gx'=32,'gy'=16] {'gy'}, dimensions={0}, use_global_device_ids=true | all-gather | bytes 139264 | tf_op jit(solution)/shard_map/all_gather | solution.py:15
  452.0 0.6 while.55
  452.9 0.7 broadcast_add_fusion
  (217 shorter events, 10.2 us)
Async XLA Ops:
  6.5 79.5 %all-gather.15.cloned.1.call-start = ((), (), s32[]{:S(2)}) async-start(), calls=%async_computation.4 | async-start | bytes 2162688 | tf_op jit(solution)/shard_map/all_gather | solution.py:15
  8.8 148.1 %copy-start = (f32[2,2,4,32,256]{4,3,2,1,0:T(8,128)S(1)}, f32[2,2,4,32,256]{4,3,2,1,0:T(8,128)}, u32[]{:S(2)}) copy-start(f32[2,2,4,32,256]{4,3,2,1,0:T(8,128)} %param.15) | copy-start | bytes 1572868
  9.6 147.2 %all-gather.13.cloned.1.call-start = ((), (), s32[]{:S(2)}) async-start(), calls=%async_computation.3 | async-start | bytes 2162688 | tf_op jit(solution)/shard_map/all_gather | solution.py:15
  10.5 243.3 %all-gather.19.cloned.1.call-start = ((), (), s32[]{:S(2)}) async-start(), calls=%async_computation.6 | async-start | bytes 2162688 | tf_op jit(solution)/shard_map/all_gather | solution.py:15
  157.1 1.8 copy-start.3
  157.1 35.5 %copy-start.2 = (s32[1,1,32,8]{2,3,1,0:T(8,128)S(1)}, s32[1,1,32,8]{2,3,1,0:T(8,128)}, u32[]{:S(2)}) copy-start(s32[1,1,32,8]{2,3,1,0:T(8,128)} %param.19) | copy-start | bytes 3076
  158.0 165.6 %all-gather.17.cloned.1.call-start = ((), (), s32[]{:S(2)}) async-start(), calls=%async_computation.5 | async-start | bytes 2162688 | tf_op jit(solution)/shard_map/all_gather | solution.py:15
  159.6 45.5 %all-to-all-start.1 = ((s32[32,1,1]{2,1,0:T(1,128)}), s32[32,1,1]{2,1,0:T(1,128)S(1)}, u32[]{:S(2)}, u32[]{:S(2)}) async-start(s32[32,1,1]{2,1,0:T(1,128)} %copy.19), calls=%async_computation.1 | async-start | bytes 32768 | tf_op jit(solution)/shard_map/all_to_all | solution.py:78
  220.5 22.4 %all-to-all-start.2 = ((f32[32,8,128]{2,1,0:T(8,128)}), f32[32,8,128]{2,1,0:T(8,128)S(1)}, u32[]{:S(2)}, u32[]{:S(2)}) async-start(f32[32,8,128]{2,1,0:T(8,128)} %bitcast.20), calls=%async_computation.2 | async-start | bytes 262144 | tf_op jit(solution)/shard_map/all_to_all | solution.py:74
  406.7 46.1 %copy-start.1 = (f32[4,32,256]{2,1,0:T(8,128)S(1)}, f32[4,32,256]{2,1,0:T(8,128)}, u32[]{:S(2)}) copy-start(f32[4,32,256]{2,1,0:T(8,128)} %param.16) | copy-start | bytes 393220
Sparse Core Ops, SparseCore 0:
  9.8 76.2 all-gather.14
  88.1 68.6 all-gather.12
  159.0 94.7 all-gather.18
  255.8 67.7 all-gather.16
where the time goes:
time: 462 us; the launch traced here: 460 us
  waiting for transfers between devices  254 us (55%)
  blocking collectives  106 us (23%)
  starting transfers between devices  37 us (8%)
  other arithmetic  36.1 us (8%)
  between operations  14.6 us (3%)
  local copies, waits for them, and re-layouts  10.7 us (2%)
    all_gather x4, waiting for transfers between devices, carried_in(): gathered = jax.tree.map(lambda a: lax.all_gather(a, axis), part)  226 us
    all_gather x4, blocking collectives, carried_in(): gathered = jax.tree.map(lambda a: lax.all_gather(a, axis), part)  90.4 us
    all_to_all x1, starting transfers between devices, on_device(): lax.all_to_all(active_packet_tally[0, 0], 'gx', split_axis=0, concat_axis...  33 us
    add x56, other arithmetic, compose(): return (earlier[0] * later[0], later[0] * earlier[1] + later[1])  28.7 us
    all_to_all x1, waiting for transfers between devices, on_device(): lax.all_to_all(deposited_packets[0, 0], 'gx', split_axis=0, concat_axis=0...  15.5 us
    all_to_all x1, blocking collectives, on_device(): lax.all_to_all(receiving_packet_position[0, 0], 'gx', split_axis=0, conca...  15.4 us
    all_to_all x1, waiting for transfers between devices, on_device(): lax.all_to_all(active_packet_tally[0, 0], 'gx', split_axis=0, concat_axis...  12.3 us
  transfers between devices with their start and end apart: 6, of which 6 were waited for; matrix products, arithmetic and copies ran while one was open for 1% of the time, Pallas kernels for 0%

commit v1 on v0

v1 whole, which is shorter than its diff:
```python
import jax
import jax.numpy as jnp
from jax import lax
from jax.experimental import pallas as pl
from jax.experimental.pallas import tpu as pltpu
from jax.sharding import PartitionSpec as P

MESH = pl.DeviceIdType.MESH
L = 128
interval_duration = 0.5
intrinsic_sq = 0.01
trap_level = 0.1


def kernel(
    c_in, w_in, tau_in, pk_in, cnt_in, site_in, out,
    C, WX, WY, TAU, SITE, CNT,
    psend, seg, xsend, xrecv, rsend, rrecv, esend, ent,
    X, WT, PT, SY, HY, GY, ysend, yrecv, zsend, zrecv,
    smsg, srecv, precv, OUT,
    in_sem, send_sem, recv_sem,
):
    nx = lax.axis_size("gx")
    ny = lax.axis_size("gy")
    nc = nx // 2
    gx = lax.axis_index("gx")
    gy = lax.axis_index("gy")
    q = lax.rem(gx, 2)
    o = 1 - q
    chip = lax.div(gx, 2)
    sub = lax.broadcasted_iota(jnp.int32, (8, L), 0)
    low = sub < 4

    def load(src, dst, i):
        copy = pltpu.make_async_copy(src, dst, in_sem.at[i])
        copy.start()
        return copy

    half = [pl.ds(h * L, L) for h in range(2)]
    first = [load(w_in.at[0, :, half[h]], WX.at[h], h) for h in range(2)]
    first += [load(c_in.at[:, half[h]], C.at[h], 2 + h) for h in range(2)]
    small = [load(site_in, SITE, 4), load(cnt_in, CNT, 5)]
    later = [load(w_in.at[1, :, half[h]], WY.at[h], 6 + h) for h in range(2)]
    last = [load(tau_in.at[:, half[h]], TAU.at[h], 8 + h) for h in range(2)]
    last += [load(pk_in.at[gx], precv.at[gx], 10)]

    barrier = pltpu.get_barrier_semaphore()

    def greet_x(r, z):
        pl.semaphore_signal(
            barrier, inc=1, device_id={"gx": lax.rem(gx + r, nx)}, device_id_type=MESH
        )
        return z

    def greet_y(r, z):
        pl.semaphore_signal(
            barrier, inc=1, device_id={"gy": lax.rem(gy + r, ny)}, device_id_type=MESH
        )
        return z

    lax.fori_loop(1, nx, greet_x, 0)
    lax.fori_loop(1, ny, greet_y, 0)

    def remote(src, dst, i, dev):
        return pltpu.make_async_remote_copy(
            src_ref=src, dst_ref=dst, send_sem=send_sem.at[i], recv_sem=recv_sem.at[i],
            device_id=dev, device_id_type=MESH,
        )

    def take(ref, sem):
        pltpu.make_async_copy(ref, ref, sem).wait()

    for copy in first:
        copy.wait()

    def x_maps(k, dst):
        for h in range(2):
            for t in range(4):
                at = [
                    pl.ds(pl.multiple_of(k * 128 + (x * 32 + t * 8), 8), 8) for x in range(4)
                ]
                w = [WX[h, at[x], :] for x in range(4)]
                c = [C[h, at[x], :] for x in range(4)]
                v = [1.0 - w[x] for x in range(4)]
                f, p = [v[0] * c[0]], [w[0]]
                for x in range(1, 4):
                    f.append(v[x] * c[x] + w[x] * f[-1])
                    p.append(w[x] * p[-1])
                g, e = v[3] * f[3], v[3] * p[3]
                for x in (2, 1, 0):
                    g = v[x] * f[x] + w[x] * g
                    e = v[x] * p[x] + w[x] * e
                for s, val in enumerate((p[3], f[3], e, g)):
                    dst[s, h, pl.ds(t * 8, 8), :] = val

    x_maps(o, psend)
    pl.semaphore_wait(barrier, nx - 1 + ny - 1)
    partner = {"gx": chip * 2 + o}
    pair = remote(psend, seg.at[q], 0, partner)
    pair.start()
    x_maps(q, seg.at[q])
    pair.wait_recv()

    for h in range(2):
        for t in range(4):
            rows = pl.ds(t * 8, 8)
            a0, b0, d0, e0 = [seg[0, s, h, rows, :] for s in range(4)]
            a1, b1, d1, e1 = [seg[1, s, h, rows, :] for s in range(4)]
            a = a0 * a1
            b = a1 * b0 + b1
            d = a0 * a0 * d1 + d0
            e = a0 * (d1 * b0 + e1) + e0
            j = h * 8 + 2 * t
            xsend[j, 0:8, :] = jnp.where(low, a, pltpu.roll(b, 4, 0))
            xsend[j, 8:16, :] = jnp.where(low, d, pltpu.roll(e, 4, 0))
            xsend[j + 1, 0:8, :] = jnp.where(low, pltpu.roll(a, 4, 0), b)
            xsend[j + 1, 8:16, :] = jnp.where(low, pltpu.roll(d, 4, 0), e)

    def send_x(r, z):
        j = lax.rem(chip + r, nc)
        remote(xsend.at[j], xrecv.at[chip], 1, {"gx": j * 2 + q}).start()
        return z

    lax.fori_loop(1, nc, send_x, 0)
    xrecv[chip] = xsend[chip]

    for copy in later:
        copy.wait()
    ya, yd = [], []
    for h in range(2):
        p = None
        for y in range(32):
            w = WY[h, pl.ds(y, 8, stride=32), :]
            WT[h, y] = w
            p = w if p is None else p * w
            PT[h, y] = p
        s = e = None
        for y in range(31, -1, -1):
            w = WT[h, y]
            vp = (1.0 - w) * PT[h, y]
            s = w if s is None else s * w
            e = vp if e is None else vp + w * e
            SY[h, pl.ds(y, 8, stride=32), :] = s
            HY[h, pl.ds(y, 8, stride=32), :] = e
        for r in range(8):
            ysend[2 * r + h, 0:1, :] = s[r : r + 1, :]
            ysend[2 * r + h, 2:3, :] = e[r : r + 1, :]

    for copy in small:
        copy.wait()
    n_dst = SITE.shape[0]
    cap = SITE.shape[1]
    diag = lax.broadcasted_iota(jnp.int32, (n_dst, n_dst), 0) == lax.broadcasted_iota(
        jnp.int32, (n_dst, n_dst), 1
    )
    counts = jnp.broadcast_to(CNT[...].astype(jnp.float32), (n_dst, n_dst))
    live = jnp.sum(jnp.where(diag, counts, 0.0), axis=1, keepdims=True)
    slot = lax.broadcasted_iota(jnp.int32, (n_dst, cap), 1).astype(jnp.float32)
    coded = jnp.where(slot < live, SITE[...].astype(jnp.float32) + 1.0, 0.0)
    lane = lax.broadcasted_iota(jnp.int32, (cap, L), 1)
    place = lax.broadcasted_iota(jnp.int32, (cap, L), 0) + cap * lax.rem(gx, L // cap)
    coded = jnp.dot(
        coded, (lane == place).astype(jnp.float32), preferred_element_type=jnp.float32,
        precision=lax.Precision.HIGHEST,
    )
    for j in range(n_dst):
        smsg[j] = coded[j : j + 1, :]
    srecv[gx] = smsg[gx]

    take(xrecv.at[pl.ds(0, nc - 1)], recv_sem.at[1])
    f = jnp.zeros((4, L), jnp.float32)
    fin = []
    for j in range(nc):
        fin.append(f)
        rsend[j, 0:4, :] = f
        f = xrecv[j, 0:4, :] * f + xrecv[j, 4:8, :]
    b = jnp.zeros((4, L), jnp.float32)
    for j in range(nc - 1, -1, -1):
        rsend[j, 4:8, :] = b
        b = xrecv[j, 0:4, :] * b + (xrecv[j, 8:12, :] * fin[j] + xrecv[j, 12:16, :])

    def send_r(r, z):
        j = lax.rem(chip + r, nc)
        remote(rsend.at[j], rrecv.at[chip], 2, {"gx": j * 2 + q}).start()
        return z

    lax.fori_loop(1, nc, send_r, 0)
    rrecv[chip] = rsend[chip]

    def send_p(r, z):
        j = lax.rem(gx + r, nx)
        remote(pk_in.at[j], precv.at[gx], 3, {"gx": j}).start()
        remote(smsg.at[j], srecv.at[gx], 4, {"gx": j}).start()
        return z

    lax.fori_loop(1, nx, send_p, 0)

    take(rrecv.at[pl.ds(0, nc - 1)], recv_sem.at[2])
    for h in range(2):
        for t in range(4):
            rows = pl.ds(t * 8, 8)
            j = h * 8 + 2 * t
            u0, u1 = rrecv[j], rrecv[j + 1]
            f = jnp.where(low, u0, pltpu.roll(u1, 4, 0))
            b = jnp.where(low, pltpu.roll(u0, 4, 0), u1)
            fm = seg[0, 0, h, rows, :] * f + seg[0, 1, h, rows, :]
            bm = (
                seg[1, 0, h, rows, :] * b + seg[1, 2, h, rows, :] * fm + seg[1, 3, h, rows, :]
            )
            is0 = q == 0
            esend[0, h, rows, :] = jnp.where(is0, fm, f)
            esend[1, h, rows, :] = jnp.where(is0, b, bm)
            ent[q, 0, h, rows, :] = jnp.where(is0, f, fm)
            ent[q, 1, h, rows, :] = jnp.where(is0, bm, b)
    pair2 = remote(esend, ent.at[q], 5, partner)
    pair2.start()

    def x_apply(k):
        for h in range(2):
            for t in range(4):
                rows = pl.ds(t * 8, 8)
                at = [
                    pl.ds(pl.multiple_of(k * 128 + (x * 32 + t * 8), 8), 8) for x in range(4)
                ]
                w = [WX[h, at[x], :] for x in range(4)]
                v = [1.0 - w[x] for x in range(4)]
                f = ent[k, 0, h, rows, :]
                b = ent[k, 1, h, rows, :]
                fs = []
                for x in range(4):
                    f = v[x] * C[h, at[x], :] + w[x] * f
                    fs.append(f)
                for x in (3, 2, 1, 0):
                    b = v[x] * fs[x] + w[x] * b
                    X[h, at[x], :] = b

    x_apply(q)
    pair2.wait_recv()
    x_apply(o)

    for h in range(2):
        f = None
        fs = []
        for y in range(32):
            w = WT[h, y]
            vx = (1.0 - w) * X[h, pl.ds(y, 8, stride=32), :]
            f = vx if f is None else vx + w * f
            PT[h, y] = f
        for r in range(8):
            ysend[2 * r + h, 1:2, :] = f[r : r + 1, :]
        g = None
        for y in range(31, -1, -1):
            w = WT[h, y]
            vf = (1.0 - w) * PT[h, y]
            g = vf if g is None else vf + w * g
            GY[h, pl.ds(y, 8, stride=32), :] = g
        for r in range(8):
            ysend[2 * r + h, 3:4, :] = g[r : r + 1, :]

    def send_y(r, z):
        j = lax.rem(gy + r, ny)
        remote(ysend.at[j], yrecv.at[gy], 6, {"gy": j}).start()
        return z

    lax.fori_loop(1, ny, send_y, 0)
    yrecv[gy] = ysend[gy]
    take(yrecv.at[pl.ds(0, ny - 1)], recv_sem.at[6])

    f = jnp.zeros((1, L), jnp.float32)
    fin = []
    for j in range(ny):
        fin.append(f)
        zsend[j, 0:1, :] = f
        f = yrecv[j, 0:1, :] * f + yrecv[j, 1:2, :]
    b = jnp.zeros((1, L), jnp.float32)
    for j in range(ny - 1, -1, -1):
        zsend[j, 1:2, :] = b
        b = yrecv[j, 0:1, :] * b + (yrecv[j, 2:3, :] * fin[j] + yrecv[j, 3:4, :])

    def send_z(r, z):
        j = lax.rem(gy + r, ny)
        remote(zsend.at[j], zrecv.at[gy], 7, {"gy": j}).start()
        return z

    lax.fori_loop(1, ny, send_z, 0)
    zrecv[gy] = zsend[gy]

    for copy in last:
        copy.wait()
    take(srecv.at[pl.ds(0, nx - 1)], recv_sem.at[4])
    take(precv.at[pl.ds(0, nx - 1)], recv_sem.at[3])
    row = lax.broadcasted_iota(jnp.int32, (2 * L, L), 0)
    code = (2 * lax.rem(row, L) + lax.div(row, L) + 1).astype(jnp.float32)
    gen = None
    per = L // cap
    for m in range(nx // per):
        sites = srecv[m * per]
        for j in range(m * per + 1, (m + 1) * per):
            sites = sites + srecv[j]
        onehot = (code == sites).astype(jnp.float32)
        blocks = precv[m * per : (m + 1) * per].reshape(L, L)
        part = jnp.dot(
            onehot, blocks, preferred_element_type=jnp.float32, precision=lax.Precision.HIGHEST
        )
        gen = part if gen is None else gen + part

    take(zrecv.at[pl.ds(0, ny - 1)], recv_sem.at[7])
    for h in range(2):
        for x in range(4):
            z0, z1 = 2 * x + h, 2 * (4 + x) + h
            fn = jnp.broadcast_to(zrecv[z0, 0:1, :], (8, L))
            bn = jnp.broadcast_to(zrecv[z0, 1:2, :], (8, L))
            fp = jnp.broadcast_to(zrecv[z1, 0:1, :], (8, L))
            bp = jnp.broadcast_to(zrecv[z1, 1:2, :], (8, L))
            for t in range(4):
                i0 = pl.ds(x * 32 + t * 8, 8)
                i1 = pl.ds(128 + x * 32 + t * 8, 8)
                n = GY[h, i0, :] + HY[h, i0, :] * fn + SY[h, i0, :] * bn
                p = GY[h, i1, :] + HY[h, i1, :] * fp + SY[h, i1, :] * bp
                rate = (n * p - intrinsic_sq) / (
                    TAU[h, i0, :] * (3.0 * (n + trap_level) + (p + trap_level))
                )
                k0 = h * L + x * 32 + t * 8
                net = interval_duration * (gen[k0 : k0 + 8, :] - rate)
                OUT[h, i0, :] = n + net
                OUT[h, i1, :] = p + net
    outs = [
        pltpu.make_async_copy(OUT.at[h], out.at[:, half[h]], in_sem.at[11 + h]) for h in range(2)
    ]
    for copy in outs:
        copy.start()
    pair.wait_send()
    take(xsend.at[pl.ds(0, nc - 1)], send_sem.at[1])
    take(rsend.at[pl.ds(0, nc - 1)], send_sem.at[2])
    take(precv.at[pl.ds(0, nx - 1)], send_sem.at[3])
    take(smsg.at[pl.ds(0, nx - 1)], send_sem.at[4])
    pair2.wait_send()
    take(ysend.at[pl.ds(0, ny - 1)], send_sem.at[6])
    take(zsend.at[pl.ds(0, ny - 1)], send_sem.at[7])
    for copy in outs:
        copy.wait()


def on_device(c, w, tau, packets, tally, position):
    f32 = jnp.float32
    nx = packets.shape[2]
    cap = packets.shape[3]
    nc, ny = nx // 2, lax.axis_size("gy")
    v = lambda *s: pltpu.VMEM(s, f32)
    full = (2, 256, L)
    scratch = [
        v(*full), v(*full), v(*full), v(2, 128, L),
        pltpu.VMEM((nx, cap), jnp.int32), pltpu.VMEM((1, nx), jnp.int32),
        v(4, 2, 32, L), v(2, 4, 2, 32, L), v(nc, 16, L), v(nc, 16, L),
        v(nc, 8, L), v(nc, 8, L), v(2, 2, 32, L), v(2, 2, 2, 32, L),
        v(*full), v(2, 32, 8, L), v(2, 32, 8, L), v(*full), v(*full), v(*full),
        v(ny, 4, L), v(ny, 4, L), v(ny, 2, L), v(ny, 2, L),
        v(nx, 1, L), v(nx, 1, L), v(nx, cap, L), v(*full),
        pltpu.SemaphoreType.DMA((13,)),
        pltpu.SemaphoreType.DMA((8,)),
        pltpu.SemaphoreType.DMA((8,)),
    ]
    out = pl.pallas_call(
        kernel,
        out_shape=jax.ShapeDtypeStruct((256, 256), f32),
        in_specs=[pl.BlockSpec(memory_space=pl.ANY)] * 6,
        out_specs=pl.BlockSpec(memory_space=pl.ANY),
        scratch_shapes=scratch,
        compiler_params=pltpu.CompilerParams(
            collective_id=0, has_side_effects=True, vmem_limit_bytes=24 * 1024 * 1024
        ),
        cost_estimate=pl.CostEstimate(
            flops=40_000_000, bytes_accessed=1_500_000, transcendentals=0
        ),
        name="step",
    )(
        c.reshape(256, 256), w.reshape(2, 256, 256), tau.reshape(128, 256),
        packets.reshape(nx, cap, L), tally.reshape(1, nx), position.reshape(nx, cap),
    )
    return out.reshape(c.shape)


def solution(mesh):
    in_specs = (
        P(None, "gx", "gy", None),
        P(None, None, "gx", "gy", None),
        P("gx", "gy", None),
        P("gx", "gy", None, None, None),
        P("gx", "gy", None),
        P("gx", "gy", None, None),
    )
    return jax.shard_map(
        on_device, mesh=mesh, in_specs=in_specs, out_specs=P(None, "gx", "gy", None),
        check_vma=False,
    )
```

time: 462 us -> 56.3 us (0.12)
  the two profiles are of different devices: /device:TPU:2 before, /device:TPU:1 now
where the time goes in v1:
time: 56.3 us; the launch traced here: 56.1 us
  Pallas kernels  50.1 us (89%)
  local copies, waits for them, and re-layouts  5.92 us (11%)
    pallas_call x1, Pallas kernels, on_device(): pl.pallas_call(kernel, out_shape=jax.ShapeDtypeStruct((256, 256), f32), i...  50.1 us
    unnamed x14, local copies, waits for them, and re-layouts  5.92 us

profile of v1, /device:TPU:1, one launch (start us, length us, event | category | flops | bytes accessed | tf_op | source)
XLA Modules:
  0.0 56.1 jit_solution(14397148182605672789)
XLA Ops:
  0.0 0.0 copy-start.5
  0.0 0.7 %copy-done.5 = s32[1,1,32,8]{2,3,1,0:T(8,128)S(1)} copy-done((s32[1,1,32,8]{2,3,1,0:T(8,128)S(1)}, s32[1,1,32,8]{2,3,1,0:T(8,128)}, u32[]{:S(2)}) %copy-start.5) | copy-done | bytes 1048
  0.7 0.1 copy.7
  0.8 0.0 copy-start.4
  0.8 0.7 %copy-done.4 = s32[1,1,32]{2,1,0:T(1,128)S(1)} copy-done((s32[1,1,32]{2,1,0:T(1,128)S(1)}, s32[1,1,32]{2,1,0:T(1,128)}, u32[]{:S(2)}) %copy-start.4) | copy-done | bytes 152
  1.4 0.0 copy-start
  1.4 1.0 %copy-done = f32[2,2,4,32,256]{4,3,2,1,0:T(8,128)S(1)} copy-done((f32[2,2,4,32,256]{4,3,2,1,0:T(8,128)S(1)}, f32[2,2,4,32,256]{4,3,2,1,0:T(8,128)}, u32[]{:S(2)}) %copy-start) | copy-done | bytes 524312
  2.5 0.0 copy-start.1
  2.5 0.9 %copy-done.1 = f32[2,4,32,256]{3,2,1,0:T(8,128)S(1)} copy-done((f32[2,4,32,256]{3,2,1,0:T(8,128)S(1)}, f32[2,4,32,256]{3,2,1,0:T(8,128)}, u32[]{:S(2)}) %copy-start.1) | copy-done | bytes 262168
  3.4 0.0 copy-start.2
  3.4 0.9 %copy-done.2 = f32[4,32,256]{2,1,0:T(8,128)S(1)} copy-done((f32[4,32,256]{2,1,0:T(8,128)S(1)}, f32[4,32,256]{2,1,0:T(8,128)}, u32[]{:S(2)}) %copy-start.2) | copy-done | bytes 131096
  4.3 0.0 copy-start.3
  4.3 0.9 %copy-done.3 = f32[1,1,32,8,128]{4,3,2,1,0:T(8,128)S(1)} copy-done((f32[1,1,32,8,128]{4,3,2,1,0:T(8,128)S(1)}, f32[1,1,32,8,128]{4,3,2,1,0:T(8,128)}, u32[]{:S(2)}) %copy-start.3) | copy-done | bytes 131096
  5.2 50.1 %step.1 = f32[256,256]{1,0:T(8,128)S(1)} custom-call(f32[256,256]{1,0:T(8,128)S(1)} %bitcast.9, f32[2,256,256]{2,1,0:T(8,128)S(1)} %bitcast.8, f32[128,256]{1,0:T(8,128)S(1)} %bitcast.10, f32[32,8,128]{2,1,0:T(8,128)S(1)} %bitcast.11, s32[1,32]{1,0:T(1,128)S(1)} %bitcast.13, s32[32,8]{1,0:T(8,128)S(1)} %bitcast.12), custom_call_target="tpu_custom_call" | custom-call | flops 40000000 | bytes 1500000 | tf_op jit(solution)/shard_map/step/pallas_call | solution.py:363
  55.4 0.7 %copy.9 = f32[2,4,32,256]{3,2,1,0:T(8,128)} copy(f32[2,4,32,256]{3,2,1,0:T(8,128)S(1)} %bitcast.7) | data formatting | bytes 524288
Async XLA Ops:
  0.0 0.7 %copy-start.5 = (s32[1,1,32,8]{2,3,1,0:T(8,128)S(1)}, s32[1,1,32,8]{2,3,1,0:T(8,128)}, u32[]{:S(2)}) copy-start(s32[1,1,32,8]{2,3,1,0:T(8,128)} %param.11) | copy-start | bytes 3076
  0.8 0.7 %copy-start.4 = (s32[1,1,32]{2,1,0:T(1,128)S(1)}, s32[1,1,32]{2,1,0:T(1,128)}, u32[]{:S(2)}) copy-start(s32[1,1,32]{2,1,0:T(1,128)} %param.10) | copy-start | bytes 388
  1.4 1.0 %copy-start = (f32[2,2,4,32,256]{4,3,2,1,0:T(8,128)S(1)}, f32[2,2,4,32,256]{4,3,2,1,0:T(8,128)}, u32[]{:S(2)}) copy-start(f32[2,2,4,32,256]{4,3,2,1,0:T(8,128)} %param.7) | copy-start | bytes 1572868
  2.5 0.9 %copy-start.1 = (f32[2,4,32,256]{3,2,1,0:T(8,128)S(1)}, f32[2,4,32,256]{3,2,1,0:T(8,128)}, u32[]{:S(2)}) copy-start(f32[2,4,32,256]{3,2,1,0:T(8,128)} %param.6) | copy-start | bytes 786436
  3.4 0.9 %copy-start.2 = (f32[4,32,256]{2,1,0:T(8,128)S(1)}, f32[4,32,256]{2,1,0:T(8,128)}, u32[]{:S(2)}) copy-start(f32[4,32,256]{2,1,0:T(8,128)} %param.8) | copy-start | bytes 393220
  4.3 0.9 %copy-start.3 = (f32[1,1,32,8,128]{4,3,2,1,0:T(8,128)S(1)}, f32[1,1,32,8,128]{4,3,2,1,0:T(8,128)}, u32[]{:S(2)}) copy-start(f32[1,1,32,8,128]{4,3,2,1,0:T(8,128)} %param.9) | copy-start | bytes 393220

commit v2 on v1

v2 whole, which is shorter than its diff:
```python
import jax
import jax.numpy as jnp
from jax import lax
from jax.experimental import pallas as pl
from jax.experimental.pallas import tpu as pltpu
from jax.sharding import PartitionSpec as P

MESH = pl.DeviceIdType.MESH
L = 128
interval_duration = 0.5
intrinsic_sq = 0.01
trap_level = 0.1


def kernel(
    c_in, w_in, tau_in, pk_in, cnt_in, site_in, out,
    C, WX, WY, TAU, SITE, CNT,
    psend, seg, xsend, xrecv, rsend, rrecv, esend, ent,
    X, WT, PT, SY, HY, GY, ysend, yrecv, zsend, zrecv,
    srow, spair, smsg, srecv, pbuf, precv,
    in_sem, pair_send, pair_recv, send_sem, recv_sem,
):
    nx = lax.axis_size("gx")
    ny = lax.axis_size("gy")
    nc = nx // 2
    gx = lax.axis_index("gx")
    gy = lax.axis_index("gy")
    q = lax.rem(gx, 2)
    o = 1 - q
    chip = lax.div(gx, 2)
    partner = {"gx": chip * 2 + o}
    sub = lax.broadcasted_iota(jnp.int32, (8, L), 0)
    low = sub < 4
    half = [pl.ds(h * L, L) for h in range(2)]
    far = sorted(range(1, nc), key=lambda r: -min(r, nc - r))
    side = 4
    far_y = sorted(
        range(1, ny),
        key=lambda r: -(min(r // side, ny // side - r // side) + min(r % side, side - r % side)),
    )

    def at_chip(r):
        return lax.rem(chip + r, nc)

    def at_y(r):
        row = lax.rem(lax.div(gy, side) + r // side, ny // side)
        return row * side + lax.rem(lax.rem(gy, side) + r % side, side)

    barrier = pltpu.get_barrier_semaphore()

    def greet(dev):
        pl.semaphore_signal(barrier, inc=1, device_id=dev, device_id_type=MESH)

    def load(src, dst, i):
        copy = pltpu.make_async_copy(src, dst, in_sem.at[i])
        copy.start()
        return copy

    for r in far:
        greet({"gx": at_chip(r) * 2 + q})
    greet(partner)
    first = [load(w_in.at[0, :, half[h]], WX.at[h], h) for h in range(2)]
    first += [load(c_in.at[:, half[h]], C.at[h], 2 + h) for h in range(2)]
    for r in far_y:
        greet({"gy": at_y(r)})
    later = [load(w_in.at[1, :, half[h]], WY.at[h], 4 + h) for h in range(2)]
    small = [load(site_in, SITE, 6), load(cnt_in, CNT, 7)]
    mine = load(pk_in.at[:, q], pbuf.at[:, q], 8)
    last = [load(tau_in.at[:, half[h]], TAU.at[h], 9 + h) for h in range(2)]

    def remote(src, dst, i, dev):
        return pltpu.make_async_remote_copy(
            src_ref=src, dst_ref=dst, send_sem=send_sem.at[i], recv_sem=recv_sem.at[i],
            device_id=dev, device_id_type=MESH,
        )

    def take(ref, sem):
        pltpu.make_async_copy(ref, ref, sem).wait()

    for copy in first:
        copy.wait()

    def x_map(k, m, dst):
        h, t = lax.div(m, 4), lax.rem(m, 4)
        at = [pl.ds(pl.multiple_of(k * 128 + x * 32 + t * 8, 8), 8) for x in range(4)]
        w = [WX[h, at[x], :] for x in range(4)]
        c = [C[h, at[x], :] for x in range(4)]
        v = [1.0 - w[x] for x in range(4)]
        f, p = [v[0] * c[0]], [w[0]]
        for x in range(1, 4):
            f.append(v[x] * c[x] + w[x] * f[-1])
            p.append(w[x] * p[-1])
        g, e = v[3] * f[3], v[3] * p[3]
        for x in (2, 1, 0):
            g = v[x] * f[x] + w[x] * g
            e = v[x] * p[x] + w[x] * e
        for s, val in enumerate((p[3], f[3], e, g)):
            dst[m, s] = val

    n_part = 4
    home = lax.div(chip, n_part)
    parts = [lax.rem(home + r, n_part) for r in (2, 1, 3, 0)]
    for c4 in parts:
        for i in range(2):
            x_map(o, c4 * 2 + i, psend)
    pl.semaphore_wait(barrier, nc - 1 + 1 + ny - 1)
    pairs = []
    for i, c4 in enumerate(parts):
        two = pl.ds(c4 * 2, 2)
        pairs.append(
            pltpu.make_async_remote_copy(
                src_ref=psend.at[two], dst_ref=seg.at[q, two],
                send_sem=pair_send.at[i], recv_sem=pair_recv.at[i],
                device_id=partner, device_id_type=MESH,
            )
        )
        pairs[-1].start()
    for c4 in parts:
        for i in range(2):
            x_map(q, c4 * 2 + i, seg.at[q])

    def send_x(j):
        remote(xsend.at[j], xrecv.at[chip], 1, {"gx": j * 2 + q}).start()

    for n, c4 in enumerate(parts):
        pairs[n].wait_recv()
        for i in range(2):
            m = c4 * 2 + i
            a0, b0, d0, e0 = [seg[0, m, s] for s in range(4)]
            a1, b1, d1, e1 = [seg[1, m, s] for s in range(4)]
            a = a0 * a1
            b = a1 * b0 + b1
            d = a0 * a0 * d1 + d0
            e = a0 * (d1 * b0 + e1) + e0
            j = m * 2
            xsend[j, 0:8, :] = jnp.where(low, a, pltpu.roll(b, 4, 0))
            xsend[j, 8:16, :] = jnp.where(low, d, pltpu.roll(e, 4, 0))
            xsend[j + 1, 0:8, :] = jnp.where(low, pltpu.roll(a, 4, 0), b)
            xsend[j + 1, 8:16, :] = jnp.where(low, pltpu.roll(d, 4, 0), e)
            if n < 3:
                send_x(j)
                send_x(j + 1)
    for r in (2, 1, 3):
        send_x(home * 4 + lax.rem(lax.rem(chip, 4) + r, 4))
    xrecv[chip] = xsend[chip]

    ppair = remote(pk_in.at[:, o], pbuf.at[:, q], 0, partner)
    ppair.start()

    for copy in later:
        copy.wait()
    for h in range(2):
        p = None
        for y in range(32):
            w = WY[h, pl.ds(y, 8, stride=32), :]
            WT[h, y] = w
            p = w if p is None else p * w
            PT[h, y] = p
        s = e = None
        for y in range(31, -1, -1):
            w = WT[h, y]
            vp = (1.0 - w) * PT[h, y]
            s = w if s is None else s * w
            e = vp if e is None else vp + w * e
            SY[h, pl.ds(y, 8, stride=32), :] = s
            HY[h, pl.ds(y, 8, stride=32), :] = e
        for r in range(8):
            ysend[2 * r + h, 0:1, :] = s[r : r + 1, :]
            ysend[2 * r + h, 2:3, :] = e[r : r + 1, :]

    for copy in small:
        copy.wait()
    cap, n_dst = SITE.shape
    slot = lax.broadcasted_iota(jnp.int32, (cap, n_dst), 0)
    coded = jnp.where(slot < CNT[...], SITE[...] + 1, 0).astype(jnp.float32)
    lane = lax.broadcasted_iota(jnp.int32, (cap, L), 1)
    per = L // cap
    place = lax.broadcasted_iota(jnp.int32, (cap, L), 0) + cap * lax.rem(gx, per)
    coded = lax.dot_general(
        coded, (lane == place).astype(jnp.float32), (((0,), (0,)), ((), ())),
        preferred_element_type=jnp.float32, precision=lax.Precision.HIGHEST,
    )
    for j in range(n_dst):
        srow[j % 2, j // 2] = coded[j : j + 1, :]
    sp = remote(srow.at[o], spair, 4, partner)
    sp.start()

    take(xrecv.at[pl.ds(0, nc - 1)], recv_sem.at[1])
    f = jnp.zeros((4, L), jnp.float32)
    fin = []
    for j in range(nc):
        fin.append(f)
        rsend[j, 0:4, :] = f
        f = xrecv[j, 0:4, :] * f + xrecv[j, 4:8, :]
    b = jnp.zeros((4, L), jnp.float32)
    for j in range(nc - 1, -1, -1):
        rsend[j, 4:8, :] = b
        b = xrecv[j, 0:4, :] * b + (xrecv[j, 8:12, :] * fin[j] + xrecv[j, 12:16, :])
    for r in far:
        j = at_chip(r)
        remote(rsend.at[j], rrecv.at[chip], 2, {"gx": j * 2 + q}).start()
    rrecv[chip] = rsend[chip]

    sp.wait_recv()
    for j in range(nc):
        smsg[j] = srow[q, j] + spair[j]
    mine.wait()
    ppair.wait_recv()
    for r in far:
        j = at_chip(r)
        remote(pbuf.at[j], precv.at[chip], 3, {"gx": j * 2 + q}).start()
    for r in far:
        j = at_chip(r)
        remote(smsg.at[j], srecv.at[chip], 8, {"gx": j * 2 + q}).start()
    precv[chip] = pbuf[chip]
    srecv[chip] = smsg[chip]

    take(rrecv.at[pl.ds(0, nc - 1)], recv_sem.at[2])
    is0 = q == 0
    for m in range(8):
        u0, u1 = rrecv[2 * m], rrecv[2 * m + 1]
        f = jnp.where(low, u0, pltpu.roll(u1, 4, 0))
        b = jnp.where(low, pltpu.roll(u0, 4, 0), u1)
        fm = seg[0, m, 0] * f + seg[0, m, 1]
        bm = seg[1, m, 0] * b + seg[1, m, 2] * fm + seg[1, m, 3]
        esend[0, m] = jnp.where(is0, fm, f)
        esend[1, m] = jnp.where(is0, b, bm)
        ent[q, 0, m] = jnp.where(is0, f, fm)
        ent[q, 1, m] = jnp.where(is0, bm, b)
    pair2 = remote(esend, ent.at[q], 5, partner)
    pair2.start()

    def x_apply(k):
        for m in range(8):
            h, t = m // 4, m % 4
            at = [pl.ds(pl.multiple_of(k * 128 + x * 32 + t * 8, 8), 8) for x in range(4)]
            w = [WX[h, at[x], :] for x in range(4)]
            v = [1.0 - w[x] for x in range(4)]
            f = ent[k, 0, m]
            b = ent[k, 1, m]
            fs = []
            for x in range(4):
                f = v[x] * C[h, at[x], :] + w[x] * f
                fs.append(f)
            for x in (3, 2, 1, 0):
                b = v[x] * fs[x] + w[x] * b
                X[h, at[x], :] = b

    x_apply(q)
    pair2.wait_recv()
    x_apply(o)

    for h in range(2):
        f = None
        for y in range(32):
            w = WT[h, y]
            vx = (1.0 - w) * X[h, pl.ds(y, 8, stride=32), :]
            f = vx if f is None else vx + w * f
            PT[h, y] = f
        for r in range(8):
            ysend[2 * r + h, 1:2, :] = f[r : r + 1, :]
        g = None
        for y in range(31, -1, -1):
            w = WT[h, y]
            vf = (1.0 - w) * PT[h, y]
            g = vf if g is None else vf + w * g
            GY[h, pl.ds(y, 8, stride=32), :] = g
        for r in range(8):
            ysend[2 * r + h, 3:4, :] = g[r : r + 1, :]
    for r in far_y:
        j = at_y(r)
        remote(ysend.at[j], yrecv.at[gy], 6, {"gy": j}).start()
    yrecv[gy] = ysend[gy]
    take(yrecv.at[pl.ds(0, ny - 1)], recv_sem.at[6])
    f = jnp.zeros((1, L), jnp.float32)
    fin = []
    for j in range(ny):
        fin.append(f)
        zsend[j, 0:1, :] = f
        f = yrecv[j, 0:1, :] * f + yrecv[j, 1:2, :]
    b = jnp.zeros((1, L), jnp.float32)
    for j in range(ny - 1, -1, -1):
        zsend[j, 1:2, :] = b
        b = yrecv[j, 0:1, :] * b + (yrecv[j, 2:3, :] * fin[j] + yrecv[j, 3:4, :])
    for r in far_y:
        j = at_y(r)
        remote(zsend.at[j], zrecv.at[gy], 7, {"gy": j}).start()
    zrecv[gy] = zsend[gy]

    for copy in last:
        copy.wait()
    take(srecv.at[pl.ds(0, nc - 1)], recv_sem.at[8])
    take(precv.at[pl.ds(0, nc - 1)], recv_sem.at[3])
    row = lax.broadcasted_iota(jnp.int32, (2 * L, L), 0)
    code = (2 * lax.rem(row, L) + lax.div(row, L) + 1).astype(jnp.float32)
    gen = None
    for m in range(2):
        lo, hi = m * nc // 2, (m + 1) * nc // 2
        sites = srecv[lo]
        for j in range(lo + 1, hi):
            sites = sites + srecv[j]
        onehot = (code == sites).astype(jnp.float32)
        blocks = precv[lo:hi].reshape(L, L)
        part = jnp.dot(
            onehot, blocks, preferred_element_type=jnp.float32, precision=lax.Precision.HIGHEST
        )
        gen = part if gen is None else gen + part

    take(zrecv.at[pl.ds(0, ny - 1)], recv_sem.at[7])
    for h in range(2):
        for x in range(4):
            z0, z1 = 2 * x + h, 2 * (4 + x) + h
            fn = jnp.broadcast_to(zrecv[z0, 0:1, :], (8, L))
            bn = jnp.broadcast_to(zrecv[z0, 1:2, :], (8, L))
            fp = jnp.broadcast_to(zrecv[z1, 0:1, :], (8, L))
            bp = jnp.broadcast_to(zrecv[z1, 1:2, :], (8, L))
            for t in range(4):
                i0 = pl.ds(x * 32 + t * 8, 8)
                i1 = pl.ds(128 + x * 32 + t * 8, 8)
                n = GY[h, i0, :] + HY[h, i0, :] * fn + SY[h, i0, :] * bn
                p = GY[h, i1, :] + HY[h, i1, :] * fp + SY[h, i1, :] * bp
                rate = (n * p - intrinsic_sq) / (
                    TAU[h, i0, :] * (3.0 * (n + trap_level) + (p + trap_level))
                )
                k0 = h * L + x * 32 + t * 8
                net = interval_duration * (gen[k0 : k0 + 8, :] - rate)
                out[i0, half[h]] = n + net
                out[i1, half[h]] = p + net

    for pair in pairs:
        pair.wait_send()
    ppair.wait_send()
    sp.wait_send()
    pair2.wait_send()
    take(xsend.at[pl.ds(0, nc - 1)], send_sem.at[1])
    take(rsend.at[pl.ds(0, nc - 1)], send_sem.at[2])
    take(precv.at[pl.ds(0, nc - 1)], send_sem.at[3])
    take(smsg.at[pl.ds(0, nc - 1)], send_sem.at[8])
    take(ysend.at[pl.ds(0, ny - 1)], send_sem.at[6])
    take(zsend.at[pl.ds(0, ny - 1)], send_sem.at[7])


def on_device(c, w, tau, packets, tally, position):
    f32 = jnp.float32
    nx = packets.shape[2]
    cap = packets.shape[3]
    nc, ny = nx // 2, lax.axis_size("gy")
    v = lambda *s: pltpu.VMEM(s, f32)
    full = (2, 256, L)
    scratch = [
        v(*full), v(*full), v(*full), v(2, 128, L),
        pltpu.VMEM((cap, nx), jnp.int32), pltpu.VMEM((1, nx), jnp.int32),
        v(8, 4, 8, L), v(2, 8, 4, 8, L), v(nc, 16, L), v(nc, 16, L),
        v(nc, 8, L), v(nc, 8, L), v(2, 8, 8, L), v(2, 2, 8, 8, L),
        v(*full), v(2, 32, 8, L), v(2, 32, 8, L), v(*full), v(*full), v(*full),
        v(ny, 4, L), v(ny, 4, L), v(ny, 2, L), v(ny, 2, L),
        v(2, nc, 1, L), v(nc, 1, L), v(nc, 1, L), v(nc, 1, L),
        v(nc, 2, cap, L), v(nc, 2, cap, L),
        pltpu.SemaphoreType.DMA((11,)),
        pltpu.SemaphoreType.DMA((4,)),
        pltpu.SemaphoreType.DMA((4,)),
        pltpu.SemaphoreType.DMA((9,)),
        pltpu.SemaphoreType.DMA((9,)),
    ]
    out = pl.pallas_call(
        kernel,
        out_shape=pltpu.VMEM((256, 256), f32),
        in_specs=[pl.BlockSpec(memory_space=pl.ANY)] * 6,
        out_specs=pl.BlockSpec(memory_space=pltpu.VMEM),
        scratch_shapes=scratch,
        compiler_params=pltpu.CompilerParams(
            collective_id=0, has_side_effects=True, vmem_limit_bytes=63 * 1024 * 1024
        ),
        cost_estimate=pl.CostEstimate(
            flops=40_000_000, bytes_accessed=1_500_000, transcendentals=0
        ),
        name="step",
    )(
        c.reshape(256, 256), w.reshape(2, 256, 256), tau.reshape(128, 256),
        packets.reshape(nc, 2, cap, L), tally.reshape(1, nx), jnp.swapaxes(position, 2, 3).reshape(cap, nx),
    )
    return out.reshape(c.shape)


def solution(mesh):
    in_specs = (
        P(None, "gx", "gy", None),
        P(None, None, "gx", "gy", None),
        P("gx", "gy", None),
        P("gx", "gy", None, None, None),
        P("gx", "gy", None),
        P("gx", "gy", None, None),
    )
    return jax.shard_map(
        on_device, mesh=mesh, in_specs=in_specs, out_specs=P(None, "gx", "gy", None),
        check_vma=False,
    )
```

time: 56.3 us -> 45.3 us (0.80)
  Pallas kernels: 50.1 us -> 44 us
  local copies, waits for them, and re-layouts: 5.92 us -> 0.71 us
    pallas_call x1, Pallas kernels: 50.1 us -> 44 us  [on_device(): pl.pallas_call(kernel, out_shape=pltpu.VMEM((256, 256), f32), in_specs=[p...]
    unnamed x14 -> x1, local copies, waits for them, and re-layouts: 5.92 us -> 0.71 us
where the time goes in v2:
time: 45.3 us; the launch traced here: 44.8 us
  Pallas kernels  44 us (97%)
  local copies, waits for them, and re-layouts  0.71 us (2%)
    pallas_call x1, Pallas kernels, on_device(): pl.pallas_call(kernel, out_shape=pltpu.VMEM((256, 256), f32), in_specs=[p...  44 us

profile of v2, /device:TPU:1, one launch (start us, length us, event | category | flops | bytes accessed | tf_op | source)
XLA Modules:
  0.0 44.8 jit_solution(8510281172487975228)
XLA Ops:
  0.0 44.0 %step.1 = f32[256,256]{1,0:T(8,128)S(1)} custom-call(f32[256,256]{1,0:T(8,128)} %bitcast.11, f32[2,256,256]{2,1,0:T(8,128)} %bitcast.10, f32[128,256]{1,0:T(8,128)} %bitcast.12, f32[16,2,8,128]{3,2,1,0:T(8,128)} %bitcast.13, s32[1,32]{1,0:T(1,128)} %bitcast.15, s32[8,32]{1,0:T(8,128)} %bitcast.14), custom_call_target="tpu_custom_call" | custom-call | flops 40000000 | bytes 1500000 | tf_op jit(solution)/shard_map/step/pallas_call | solution.py:365
  44.0 0.7 %copy.8 = f32[2,4,32,256]{3,2,1,0:T(8,128)} copy(f32[2,4,32,256]{3,2,1,0:T(8,128)S(1)} %bitcast.9) | data formatting | bytes 524288

commit v3 on v2

--- a/solution.py
+++ b/solution.py
@@ -15,10 +15,10 @@
 def kernel(
     c_in, w_in, tau_in, pk_in, cnt_in, site_in, out,
     C, WX, WY, TAU, SITE, CNT,
-    psend, seg, xsend, xrecv, rsend, rrecv, esend, ent,
-    X, WT, PT, SY, HY, GY, ysend, yrecv, zsend, zrecv,
-    srow, spair, smsg, srecv, pbuf, precv,
-    in_sem, pair_send, pair_recv, send_sem, recv_sem,
+    psend, seg, xsend, xrecv, rsend, rrecv, WX2, C2,
+    X, WT, PT, SY, HY, GY, SR, HR, GR, ysend, yrecv, fb,
+    srow, spair, pbuf, precv,
+    in_sem, pair_send, pair_recv, send_sem, recv_sem, hand,
 ):
     nx = lax.axis_size("gx")
     ny = lax.axis_size("gy")
@@ -57,16 +57,26 @@
         return copy
 
     for r in far:
-        greet({"gx": at_chip(r) * 2 + q})
-    greet(partner)
+        greet({"gx": at_chip(r) * 2})
+
+    @pl.when(q == 0)
+    def _():
+        greet(partner)
+
     first = [load(w_in.at[0, :, half[h]], WX.at[h], h) for h in range(2)]
     first += [load(c_in.at[:, half[h]], C.at[h], 2 + h) for h in range(2)]
     for r in far_y:
-        greet({"gy": at_y(r)})
-    later = [load(w_in.at[1, :, half[h]], WY.at[h], 4 + h) for h in range(2)]
+        greet({"gx": chip * 2, "gy": at_y(r)})
+
+    def signal_partner():
+        pl.semaphore_signal(hand, inc=1, device_id=partner, device_id_type=MESH)
+
+    own, other = pl.ds(q * 128, 128), pl.ds(o * 128, 128)
+    later = [load(w_in.at[1, own, half[h]], WY.at[h, own], 4 + h) for h in range(2)]
     small = [load(site_in, SITE, 6), load(cnt_in, CNT, 7)]
-    mine = load(pk_in.at[:, q], pbuf.at[:, q], 8)
+    mine = load(pk_in.at[:, q], pbuf.at[:, pl.ds(q * 8, 8)], 8)
     last = [load(tau_in.at[:, half[h]], TAU.at[h], 9 + h) for h in range(2)]
+    again = [load(w_in.at[0, own], WX2.at[q], 11), load(c_in.at[own], C2.at[q], 12)]
 
     def remote(src, dst, i, dev):
         return pltpu.make_async_remote_copy(
@@ -103,7 +113,15 @@
     for c4 in parts:
         for i in range(2):
             x_map(o, c4 * 2 + i, psend)
-    pl.semaphore_wait(barrier, nc - 1 + 1 + ny - 1)
+    @pl.when(q == 0)
+    def _():
+        pl.semaphore_wait(hand, 1)
+
+    @pl.when(q == 1)
+    def _():
+        pl.semaphore_wait(barrier, 1)
+        signal_partner()
+
     pairs = []
     for i, c4 in enumerate(parts):
         two = pl.ds(c4 * 2, 2)
@@ -137,18 +155,47 @@
             xsend[j, 8:16, :] = jnp.where(low, d, pltpu.roll(e, 4, 0))
             xsend[j + 1, 0:8, :] = jnp.where(low, pltpu.roll(a, 4, 0), b)
             xsend[j + 1, 8:16, :] = jnp.where(low, pltpu.roll(d, 4, 0), e)
-            if n < 3:
-                send_x(j)
-                send_x(j + 1)
-    for r in (2, 1, 3):
-        send_x(home * 4 + lax.rem(lax.rem(chip, 4) + r, 4))
+
+    swaps = [remote(w_in.at[1, other, half[h]], WY.at[h, own], 9 + h, partner) for h in range(2)]
+    swaps += [
+        remote(w_in.at[0, other], WX2.at[q], 11, partner),
+        remote(c_in.at[other], C2.at[q], 12, partner),
+        remote(pk_in.at[:, o], pbuf.at[:, pl.ds(q * 8, 8)], 0, partner),
+    ]
+    for swap in swaps:
+        swap.start()
+
+    @pl.when(q == 0)
+    def _():
+        pl.semaphore_wait(barrier, 2 * (nc - 1 + ny - 1))
+        signal_partner()
+
+    @pl.when(q == 1)
+    def _():
+        pl.semaphore_wait(hand, 1)
+
+    for r in far:
+        send_x(at_chip(r))
     xrecv[chip] = xsend[chip]
 
-    ppair = remote(pk_in.at[:, o], pbuf.at[:, q], 0, partner)
-    ppair.start()
+    def y_pack(i, h, u, v):
+        ysend[i, 0, h] = jnp.where(low, u, pltpu.roll(v, 4, 0))
+        ysend[i, 1, h] = jnp.where(low, pltpu.roll(u, 4, 0), v)
+
+    def y_share(i, sem):
+        spot = gy * 2 + q
+        for r in far_y:
+            j = at_y(r)
+            for c in range(2):
+                dev = {"gx": chip * 2 + c, "gy": j}
+                remote(ysend.at[i, c], yrecv.at[i, spot], sem, dev).start()
+        remote(ysend.at[i, o], yrecv.at[i, spot], sem, partner).start()
+        yrecv[i, spot] = ysend[i, q]
 
     for copy in later:
         copy.wait()
+    for swap in swaps[:2]:
+        swap.wait_recv()
     for h in range(2):
         p = None
         for y in range(32):
@@ -164,9 +211,12 @@
             e = vp if e is None else vp + w * e
             SY[h, pl.ds(y, 8, stride=32), :] = s
             HY[h, pl.ds(y, 8, stride=32), :] = e
-        for r in range(8):
-            ysend[2 * r + h, 0:1, :] = s[r : r + 1, :]
-            ysend[2 * r + h, 2:3, :] = e[r : r + 1, :]
+        y_pack(0, h, s, e)
+
+    hs = [remote(SY.at[:, other], SR, 13, partner), remote(HY.at[:, other], HR, 14, partner)]
+    for swap in hs:
+        swap.start()
+    y_share(0, 7)
 
     for copy in small:
         copy.wait()
@@ -185,6 +235,16 @@
     sp = remote(srow.at[o], spair, 4, partner)
     sp.start()
 
+    mine.wait()
+    swaps[4].wait_recv()
+    sp.wait_recv()
+    for j in range(nc):
+        pbuf[j, 16:17, :] = srow[q, j] + spair[j]
+    precv[chip] = pbuf[chip]
+    for r in far[8:]:
+        j = at_chip(r)
+        remote(pbuf.at[j], precv.at[chip], 3, {"gx": j * 2 + q}).start()
+
     take(xrecv.at[pl.ds(0, nc - 1)], recv_sem.at[1])
     f = jnp.zeros((4, L), jnp.float32)
     fin = []
@@ -201,54 +261,31 @@
         remote(rsend.at[j], rrecv.at[chip], 2, {"gx": j * 2 + q}).start()
     rrecv[chip] = rsend[chip]
 
-    sp.wait_recv()
-    for j in range(nc):
-        smsg[j] = srow[q, j] + spair[j]
-    mine.wait()
-    ppair.wait_recv()
-    for r in far:
+    for copy in again:
+        copy.wait()
+    for swap in swaps[2:4]:
+        swap.wait_recv()
+    take(rrecv.at[pl.ds(0, nc - 1)], recv_sem.at[2])
+
+    for r in far[:8]:
         j = at_chip(r)
         remote(pbuf.at[j], precv.at[chip], 3, {"gx": j * 2 + q}).start()
-    for r in far:
-        j = at_chip(r)
-        remote(smsg.at[j], srecv.at[chip], 8, {"gx": j * 2 + q}).start()
-    precv[chip] = pbuf[chip]
-    srecv[chip] = smsg[chip]
-
-    take(rrecv.at[pl.ds(0, nc - 1)], recv_sem.at[2])
-    is0 = q == 0
+
     for m in range(8):
+        h, t = m // 4, m % 4
         u0, u1 = rrecv[2 * m], rrecv[2 * m + 1]
         f = jnp.where(low, u0, pltpu.roll(u1, 4, 0))
         b = jnp.where(low, pltpu.roll(u0, 4, 0), u1)
-        fm = seg[0, m, 0] * f + seg[0, m, 1]
-        bm = seg[1, m, 0] * b + seg[1, m, 2] * fm + seg[1, m, 3]
-        esend[0, m] = jnp.where(is0, fm, f)
-        esend[1, m] = jnp.where(is0, b, bm)
-        ent[q, 0, m] = jnp.where(is0, f, fm)
-        ent[q, 1, m] = jnp.where(is0, bm, b)
-    pair2 = remote(esend, ent.at[q], 5, partner)
-    pair2.start()
-
-    def x_apply(k):
-        for m in range(8):
-            h, t = m // 4, m % 4
-            at = [pl.ds(pl.multiple_of(k * 128 + x * 32 + t * 8, 8), 8) for x in range(4)]
-            w = [WX[h, at[x], :] for x in range(4)]
-            v = [1.0 - w[x] for x in range(4)]
-            f = ent[k, 0, m]
-            b = ent[k, 1, m]
-            fs = []
-            for x in range(4):
-                f = v[x] * C[h, at[x], :] + w[x] * f
-                fs.append(f)
-            for x in (3, 2, 1, 0):
-                b = v[x] * fs[x] + w[x] * b
-                X[h, at[x], :] = b
-
-    x_apply(q)
-    pair2.wait_recv()
-    x_apply(o)
+        at = [(x // 4, pl.ds((x % 4) * 32 + t * 8, 8), half[h]) for x in range(8)]
+        w = [WX2[i] for i in at]
+        v = [1.0 - w[x] for x in range(8)]
+        fs = []
+        for x in range(8):
+            f = v[x] * C2[at[x]] + w[x] * f
+            fs.append(f)
+        for x in range(7, -1, -1):
+            b = v[x] * fs[x] + w[x] * b
+            X[h, pl.ds(x * 32 + t * 8, 8), :] = b
 
     for h in range(2):
         f = None
@@ -257,87 +294,82 @@
             vx = (1.0 - w) * X[h, pl.ds(y, 8, stride=32), :]
             f = vx if f is None else vx + w * f
             PT[h, y] = f
-        for r in range(8):
-            ysend[2 * r + h, 1:2, :] = f[r : r + 1, :]
+        last_f = f
         g = None
         for y in range(31, -1, -1):
             w = WT[h, y]
             vf = (1.0 - w) * PT[h, y]
             g = vf if g is None else vf + w * g
             GY[h, pl.ds(y, 8, stride=32), :] = g
-        for r in range(8):
-            ysend[2 * r + h, 3:4, :] = g[r : r + 1, :]
-    for r in far_y:
-        j = at_y(r)
-        remote(ysend.at[j], yrecv.at[gy], 6, {"gy": j}).start()
-    yrecv[gy] = ysend[gy]
-    take(yrecv.at[pl.ds(0, ny - 1)], recv_sem.at[6])
-    f = jnp.zeros((1, L), jnp.float32)
-    fin = []
-    for j in range(ny):
-        fin.append(f)
-        zsend[j, 0:1, :] = f
-        f = yrecv[j, 0:1, :] * f + yrecv[j, 1:2, :]
-    b = jnp.zeros((1, L), jnp.float32)
-    for j in range(ny - 1, -1, -1):
-        zsend[j, 1:2, :] = b
-        b = yrecv[j, 0:1, :] * b + (yrecv[j, 2:3, :] * fin[j] + yrecv[j, 3:4, :])
-    for r in far_y:
-        j = at_y(r)
-        remote(zsend.at[j], zrecv.at[gy], 7, {"gy": j}).start()
-    zrecv[gy] = zsend[gy]
-
+        y_pack(1, h, last_f, g)
+    y_share(1, 6)
+    gs = remote(GY.at[:, other], GR, 15, partner)
+    gs.start()
+    for swap in hs:
+        swap.wait_recv()
+    take(yrecv.at[0, pl.ds(0, 2 * ny - 1)], recv_sem.at[7])
+    take(yrecv.at[1, pl.ds(0, 2 * ny - 1)], recv_sem.at[6])
+    for k in range(2):
+        for h in range(2):
+            f = jnp.zeros((4, L), jnp.float32)
+            fin = []
+            for j in range(ny):
+                fin.append(f)
+                fb[j, k, h, 0:4, :] = f
+                f = yrecv[0, 2 * j + k, h, 0:4, :] * f + yrecv[1, 2 * j + k, h, 0:4, :]
+            b = jnp.zeros((4, L), jnp.float32)
+            for j in range(ny - 1, -1, -1):
+                fb[j, k, h, 4:8, :] = b
+                e = yrecv[0, 2 * j + k, h, 4:8, :] * fin[j] + yrecv[1, 2 * j + k, h, 4:8, :]
+                b = yrecv[0, 2 * j + k, h, 0:4, :] * b + e
+    gs.wait_recv()
     for copy in last:
         copy.wait()
-    take(srecv.at[pl.ds(0, nc - 1)], recv_sem.at[8])
     take(precv.at[pl.ds(0, nc - 1)], recv_sem.at[3])
     row = lax.broadcasted_iota(jnp.int32, (2 * L, L), 0)
     code = (2 * lax.rem(row, L) + lax.div(row, L) + 1).astype(jnp.float32)
     gen = None
     for m in range(2):
         lo, hi = m * nc // 2, (m + 1) * nc // 2
-        sites = srecv[lo]
+        sites = precv[lo, 16:17, :]
         for j in range(lo + 1, hi):
-            sites = sites + srecv[j]
+            sites = sites + precv[j, 16:17, :]
         onehot = (code == sites).astype(jnp.float32)
-        blocks = precv[lo:hi].reshape(L, L)
+        blocks = precv[lo:hi, 0:16, :].reshape(L, L)
         part = jnp.dot(
             onehot, blocks, preferred_element_type=jnp.float32, precision=lax.Precision.HIGHEST
         )
         gen = part if gen is None else gen + part
 
-    take(zrecv.at[pl.ds(0, ny - 1)], recv_sem.at[7])
+    is0 = q == 0
     for h in range(2):
         for x in range(4):
-            z0, z1 = 2 * x + h, 2 * (4 + x) + h
-            fn = jnp.broadcast_to(zrecv[z0, 0:1, :], (8, L))
-            bn = jnp.broadcast_to(zrecv[z0, 1:2, :], (8, L))
-            fp = jnp.broadcast_to(zrecv[z1, 0:1, :], (8, L))
-            bp = jnp.broadcast_to(zrecv[z1, 1:2, :], (8, L))
+            f0 = jnp.broadcast_to(fb[gy, q, h, x : x + 1, :], (8, L))
+            b0 = jnp.broadcast_to(fb[gy, q, h, 4 + x : 5 + x, :], (8, L))
+            f1 = jnp.broadcast_to(fb[gy, o, h, x : x + 1, :], (8, L))
+            b1 = jnp.broadcast_to(fb[gy, o, h, 4 + x : 5 + x, :], (8, L))
             for t in range(4):
-                i0 = pl.ds(x * 32 + t * 8, 8)
-                i1 = pl.ds(128 + x * 32 + t * 8, 8)
-                n = GY[h, i0, :] + HY[h, i0, :] * fn + SY[h, i0, :] * bn
-                p = GY[h, i1, :] + HY[h, i1, :] * fp + SY[h, i1, :] * bp
+                i = pl.ds(x * 32 + t * 8, 8)
+                i0 = pl.ds(pl.multiple_of(q * 128 + x * 32 + t * 8, 8), 8)
+                i1 = pl.ds(pl.multiple_of(o * 128 + x * 32 + t * 8, 8), 8)
+                u0 = GY[h, i0, :] + HY[h, i0, :] * f0 + SY[h, i0, :] * b0
+                u1 = GR[h, i, :] + HR[h, i, :] * f1 + SR[h, i, :] * b1
+                n, p = jnp.where(is0, u0, u1), jnp.where(is0, u1, u0)
                 rate = (n * p - intrinsic_sq) / (
-                    TAU[h, i0, :] * (3.0 * (n + trap_level) + (p + trap_level))
+                    TAU[h, i, :] * (3.0 * (n + trap_level) + (p + trap_level))
                 )
                 k0 = h * L + x * 32 + t * 8
                 net = interval_duration * (gen[k0 : k0 + 8, :] - rate)
-                out[i0, half[h]] = n + net
-                out[i1, half[h]] = p + net
-
-    for pair in pairs:
-        pair.wait_send()
-    ppair.wait_send()
-    sp.wait_send()
-    pair2.wait_send()
+                out[i0, half[h]] = u0 + net
+                out[i1, half[h]] = u1 + net
+
+    for copy in pairs + swaps + hs + [sp, gs]:
+        copy.wait_send()
     take(xsend.at[pl.ds(0, nc - 1)], send_sem.at[1])
     take(rsend.at[pl.ds(0, nc - 1)], send_sem.at[2])
     take(precv.at[pl.ds(0, nc - 1)], send_sem.at[3])
-    take(smsg.at[pl.ds(0, nc - 1)], send_sem.at[8])
-    take(ysend.at[pl.ds(0, ny - 1)], send_sem.at[6])
-    take(zsend.at[pl.ds(0, ny - 1)], send_sem.at[7])
+    take(yrecv.at[0, pl.ds(0, 2 * ny - 1)], send_sem.at[7])
+    take(yrecv.at[1, pl.ds(0, 2 * ny - 1)], send_sem.at[6])
 
 
 def on_device(c, w, tau, packets, tally, position):
@@ -351,16 +383,18 @@
         v(*full), v(*full), v(*full), v(2, 128, L),
         pltpu.VMEM((cap, nx), jnp.int32), pltpu.VMEM((1, nx), jnp.int32),
         v(8, 4, 8, L), v(2, 8, 4, 8, L), v(nc, 16, L), v(nc, 16, L),
-        v(nc, 8, L), v(nc, 8, L), v(2, 8, 8, L), v(2, 2, 8, 8, L),
+        v(nc, 8, L), v(nc, 8, L), v(2, 128, 256), v(2, 128, 256),
         v(*full), v(2, 32, 8, L), v(2, 32, 8, L), v(*full), v(*full), v(*full),
-        v(ny, 4, L), v(ny, 4, L), v(ny, 2, L), v(ny, 2, L),
-        v(2, nc, 1, L), v(nc, 1, L), v(nc, 1, L), v(nc, 1, L),
-        v(nc, 2, cap, L), v(nc, 2, cap, L),
-        pltpu.SemaphoreType.DMA((11,)),
+        v(2, 128, L), v(2, 128, L), v(2, 128, L),
+        v(2, 2, 2, 8, L), v(2, 2 * ny, 2, 8, L), v(ny, 2, 2, 8, L),
+        v(2, nc, 1, L), v(nc, 1, L),
+        v(nc, 2 * cap + 1, L), v(nc, 2 * cap + 1, L),
+        pltpu.SemaphoreType.DMA((13,)),
         pltpu.SemaphoreType.DMA((4,)),
         pltpu.SemaphoreType.DMA((4,)),
-        pltpu.SemaphoreType.DMA((9,)),
-        pltpu.SemaphoreType.DMA((9,)),
+        pltpu.SemaphoreType.DMA((16,)),
+        pltpu.SemaphoreType.DMA((16,)),
+        pltpu.SemaphoreType.REGULAR,
     ]
     out = pl.pallas_call(
         kernel,

time: 45.3 us -> 41.1 us (0.907)
  Pallas kernels: 44 us -> 40.2 us
    pallas_call x1, Pallas kernels: 44 us -> 40.2 us  [on_device(): pl.pallas_call(kernel, out_shape=pltpu.VMEM((256, 256), f32), in_specs=[p...]
where the time goes in v3:
time: 41.1 us; the launch traced here: 40.9 us
  Pallas kernels  40.2 us (98%)
  local copies, waits for them, and re-layouts  0.71 us (2%)
    pallas_call x1, Pallas kernels, on_device(): pl.pallas_call(kernel, out_shape=pltpu.VMEM((256, 256), f32), in_specs=[p...  40.2 us

profile of v3, /device:TPU:1, one launch (start us, length us, event | category | flops | bytes accessed | tf_op | source)
XLA Modules:
  0.0 40.9 jit_solution(3233614294774926286)
XLA Ops:
  0.0 40.2 %step.1 = f32[256,256]{1,0:T(8,128)S(1)} custom-call(f32[256,256]{1,0:T(8,128)} %bitcast.11, f32[2,256,256]{2,1,0:T(8,128)} %bitcast.10, f32[128,256]{1,0:T(8,128)} %bitcast.12, f32[16,2,8,128]{3,2,1,0:T(8,128)} %bitcast.13, s32[1,32]{1,0:T(1,128)} %bitcast.15, s32[8,32]{1,0:T(8,128)} %bitcast.14), custom_call_target="tpu_custom_call" | custom-call | flops 40000000 | bytes 1500000 | tf_op jit(solution)/shard_map/step/pallas_call | solution.py:399
  40.2 0.7 %copy.8 = f32[2,4,32,256]{3,2,1,0:T(8,128)} copy(f32[2,4,32,256]{3,2,1,0:T(8,128)S(1)} %bitcast.9) | data formatting | bytes 524288

commit v4 on v3

--- a/solution.py
+++ b/solution.py
@@ -267,10 +267,6 @@
         swap.wait_recv()
     take(rrecv.at[pl.ds(0, nc - 1)], recv_sem.at[2])
 
-    for r in far[:8]:
-        j = at_chip(r)
-        remote(pbuf.at[j], precv.at[chip], 3, {"gx": j * 2 + q}).start()
-
     for m in range(8):
         h, t = m // 4, m % 4
         u0, u1 = rrecv[2 * m], rrecv[2 * m + 1]
@@ -303,6 +299,10 @@
             GY[h, pl.ds(y, 8, stride=32), :] = g
         y_pack(1, h, last_f, g)
     y_share(1, 6)
+    for r in far[:8]:
+        j = at_chip(r)
+        remote(pbuf.at[j], precv.at[chip], 3, {"gx": j * 2 + q}).start()
+
     gs = remote(GY.at[:, other], GR, 15, partner)
     gs.start()
     for swap in hs:

time: 41.1 us -> 41 us (level)
  no operation moved by 1% of the time
where the time goes in v4:
time: 41 us; the launch traced here: 40.9 us
  Pallas kernels  40.2 us (98%)
  local copies, waits for them, and re-layouts  0.71 us (2%)
    pallas_call x1, Pallas kernels, on_device(): pl.pallas_call(kernel, out_shape=pltpu.VMEM((256, 256), f32), in_specs=[p...  40.2 us

profile of v4, /device:TPU:1, one launch (start us, length us, event | category | flops | bytes accessed | tf_op | source)
XLA Modules:
  0.0 40.9 jit_solution(8356632785072025691)
XLA Ops:
  0.0 40.2 %step.1 = f32[256,256]{1,0:T(8,128)S(1)} custom-call(f32[256,256]{1,0:T(8,128)} %bitcast.11, f32[2,256,256]{2,1,0:T(8,128)} %bitcast.10, f32[128,256]{1,0:T(8,128)} %bitcast.12, f32[16,2,8,128]{3,2,1,0:T(8,128)} %bitcast.13, s32[1,32]{1,0:T(1,128)} %bitcast.15, s32[8,32]{1,0:T(8,128)} %bitcast.14), custom_call_target="tpu_custom_call" | custom-call | flops 40000000 | bytes 1500000 | tf_op jit(solution)/shard_map/step/pallas_call | solution.py:399
  40.2 0.7 %copy.8 = f32[2,4,32,256]{3,2,1,0:T(8,128)} copy(f32[2,4,32,256]{3,2,1,0:T(8,128)S(1)} %bitcast.9) | data formatting | bytes 524288

commit v5 on v4

--- a/solution.py
+++ b/solution.py
@@ -56,12 +56,12 @@
         copy.start()
         return copy
 
-    for r in far:
-        greet({"gx": at_chip(r) * 2})
-
     @pl.when(q == 0)
     def _():
         greet(partner)
+
+    for r in far:
+        greet({"gx": at_chip(r) * 2})
 
     first = [load(w_in.at[0, :, half[h]], WX.at[h], h) for h in range(2)]
     first += [load(c_in.at[:, half[h]], C.at[h], 2 + h) for h in range(2)]
@@ -184,10 +184,9 @@
 
     def y_share(i, sem):
         spot = gy * 2 + q
-        for r in far_y:
-            j = at_y(r)
-            for c in range(2):
-                dev = {"gx": chip * 2 + c, "gy": j}
+        for c in (o, q):
+            for r in far_y:
+                dev = {"gx": chip * 2 + c, "gy": at_y(r)}
                 remote(ysend.at[i, c], yrecv.at[i, spot], sem, dev).start()
         remote(ysend.at[i, o], yrecv.at[i, spot], sem, partner).start()
         yrecv[i, spot] = ysend[i, q]
@@ -214,9 +213,6 @@
         y_pack(0, h, s, e)
 
     hs = [remote(SY.at[:, other], SR, 13, partner), remote(HY.at[:, other], HR, 14, partner)]
-    for swap in hs:
-        swap.start()
-    y_share(0, 7)
 
     for copy in small:
         copy.wait()
@@ -265,6 +261,9 @@
         copy.wait()
     for swap in swaps[2:4]:
         swap.wait_recv()
+    for swap in hs:
+        swap.start()
+    y_share(0, 7)
     take(rrecv.at[pl.ds(0, nc - 1)], recv_sem.at[2])
 
     for m in range(8):

time: 41 us -> 40.9 us (level)
  no operation moved by 1% of the time
where the time goes in v5:
time: 40.9 us; the launch traced here: 40.7 us
  Pallas kernels  40 us (98%)
  local copies, waits for them, and re-layouts  0.71 us (2%)
    pallas_call x1, Pallas kernels, on_device(): pl.pallas_call(kernel, out_shape=pltpu.VMEM((256, 256), f32), in_specs=[p...  40 us

profile of v5, /device:TPU:1, one launch (start us, length us, event | category | flops | bytes accessed | tf_op | source)
XLA Modules:
  0.0 40.7 jit_solution(9725410770504825576)
XLA Ops:
  0.0 40.0 %step.1 = f32[256,256]{1,0:T(8,128)S(1)} custom-call(f32[256,256]{1,0:T(8,128)} %bitcast.11, f32[2,256,256]{2,1,0:T(8,128)} %bitcast.10, f32[128,256]{1,0:T(8,128)} %bitcast.12, f32[16,2,8,128]{3,2,1,0:T(8,128)} %bitcast.13, s32[1,32]{1,0:T(1,128)} %bitcast.15, s32[8,32]{1,0:T(8,128)} %bitcast.14), custom_call_target="tpu_custom_call" | custom-call | flops 40000000 | bytes 1500000 | tf_op jit(solution)/shard_map/step/pallas_call | solution.py:398
  40.0 0.7 %copy.8 = f32[2,4,32,256]{3,2,1,0:T(8,128)} copy(f32[2,4,32,256]{3,2,1,0:T(8,128)S(1)} %bitcast.9) | data formatting | bytes 524288
